TPU v7x, 512 devices: a whole 4x4x16 slice. The times are simulated.
512 devices in a mesh: member: 8 (over y, x_hi), space: 64 (over x_lo, z, core).
Axes of the slice: x: 4 (x_hi: 2, x_lo: 2; x = x_hi * 2 + x_lo), y: 4, z: 16, core: 2. Of those that a mesh axis runs over, the one named last changes fastest.
Arguments:
- latent: bfloat16 [16, 4096, 1024], P('member', 'space'), may hold values from -6 to 6
- edge_weight: float32 [3, 32768], P(None, 'space'), may hold values from 0.1 to 1
- neighbours: int32 [3, 32768], P(None, 'space'), may hold values from 0 to 4095, as said below
- band_rows: int32 [64], P('space'), may hold values from 1 to 512, 24576 in all
- w_in: bfloat16 [1024, 1024], replicated, may hold values from -0.1875 to 0.1875
- w_out: bfloat16 [69, 1024], replicated, may hold values from -0.1875 to 0.1875
- target: float32 [69, 32768], P(None, 'space'), may hold values from -80 to 80
Outputs:
- score: float32 [], replicated
- grad_latent: bfloat16 [16, 4096, 1024], P('member', 'space')
- grad_w_out: float32 [69, 1024], P(None, 'space')
Inputs may be any that keep to these rules, and one draw needn't show every extreme that they name: `neighbours`: the node of an edge at grid slot g lies in latitude band g // 512 or one of the two bands beside it, node band b holding nodes b * 64 to (b + 1) * 64 - 1. Band b holds real grid points in its first band_rows[b] slots and padding after them; some band is full.
All inputs are finite; a program needn't handle non-finite values. No bound on the sum of `band_rows` on one device may be relied on, other than what follows from the above.
Results may differ from a plain program's by a relative error of at most 0.0075.
Values may be sent and summed in bfloat16 or wider, within the bound.
No kernel may reach another device: no remote copies, remote signals or barrier semaphores. Data moves between devices by JAX's collectives and lax.ppermute only.
A program may use at most 64 MiB of HBM per device.

v0:
```python
import jax
import jax.numpy as jnp
from jax import lax
from jax.sharding import PartitionSpec as P

epsilon = 1e-06


def extended_2(array, sides, width):
    for axis, dim in sides:
        size, length = (lax.axis_size(axis), array.shape[dim])
        up = [(i, (i + 1) % size) for i in range(size - 1)]
        down = [(j, i) for i, j in up]
        last = lax.slice_in_dim(array, length - width, length, axis=dim)
        first = lax.slice_in_dim(array, 0, width, axis=dim)
        before = lax.ppermute(last, axis, up)
        after = lax.ppermute(first, axis, down)
        array = jnp.concatenate([before, array, after], axis=dim)
    return array


def passed_along(array, axis, by):
    length = lax.axis_size(axis)
    pairs = [(i, i + by) for i in range(length) if 0 <= i + by < length]
    return lax.ppermute(array, axis, pairs)


def partials(everyone, target_rows, valid_rows):
    deviation = everyone - target_rows[None]
    target_sums = jnp.sum(valid_rows * deviation * deviation, axis=(1, 2))

    def against(member_field):
        spread = everyone - member_field[None]
        return jnp.sum(valid_rows * spread * spread, axis=(1, 2))

    pair_sums = lax.map(against, everyone)
    return (target_sums, pair_sums, jnp.sum(valid_rows))


def finish(target_sums, pair_sums, cell_count, variables):
    members = target_sums.shape[0]
    cells = variables * cell_count
    target_dist = jnp.sqrt(target_sums / cells + epsilon)
    pair_dist = jnp.sqrt(pair_sums / cells + epsilon)
    apart = 1.0 - jnp.eye(members, dtype=jnp.float32)
    pair_coef = apart / pair_dist
    score = jnp.mean(target_dist) - jnp.sum(apart * pair_dist) / (2.0 * members * (members - 1))
    return (score, pair_coef, target_dist)


def member_grads(chosen, everyone, coef_rows, dist_rows, target_rows, valid_rows):
    members = everyone.shape[0]
    others = jnp.sum(coef_rows[:, :, None, None] * everyone[None], axis=1)
    spread = jnp.sum(coef_rows, axis=1)[:, None, None] * chosen - others
    toward = (chosen - target_rows[None]) / (members * dist_rows[:, None, None])
    return (valid_rows * (toward - spread / (members * (members - 1)))).astype(jnp.bfloat16)


def per_device(latent, edge_weight, neighbours, band_rows, w_in, w_out, target):
    members_dev, nodes_dev, latent_width = latent.shape
    neigh_count, row_count = edge_weight.shape
    variables = w_out.shape[0]
    band_index = lax.axis_index("space")
    extended = extended_2(latent, (("space", 1),), nodes_dev)
    local_index = neighbours - (band_index - 1) * nodes_dev
    picked = jnp.take(extended, local_index.reshape(-1), axis=1).reshape(
        members_dev, neigh_count, row_count, latent_width
    )
    aggregated = edge_weight[0][None, :, None] * picked[:, 0].astype(jnp.float32)
    for neighbour in range(1, neigh_count):
        aggregated = aggregated + edge_weight[neighbour][None, :, None] * picked[
            :, neighbour
        ].astype(jnp.float32)
    latent_mix = aggregated.astype(jnp.bfloat16)
    preact = jnp.einsum("mgd,de->mge", latent_mix, w_in, preferred_element_type=jnp.float32)
    hidden = jax.nn.silu(preact).astype(jnp.bfloat16)
    fields = jnp.einsum("vd,mgd->mvg", w_out, hidden, preferred_element_type=jnp.float32).astype(
        jnp.bfloat16
    )
    valid_rows = (jnp.arange(row_count) < band_rows[0]).astype(jnp.float32)
    everyone = lax.all_gather(fields, "member", axis=0, tiled=True).astype(jnp.float32)
    target_sums, pair_sums, cell_count = partials(everyone, target, valid_rows)
    target_sums, pair_sums, cell_count = lax.psum((target_sums, pair_sums, cell_count), "space")
    score, pair_coef, target_dist = finish(target_sums, pair_sums, cell_count, variables)
    first_member = lax.axis_index("member") * members_dev
    coef_rows = lax.dynamic_slice_in_dim(pair_coef, first_member, members_dev, 0)
    dist_rows = lax.dynamic_slice_in_dim(target_dist, first_member, members_dev, 0)
    grad_fields = member_grads(
        fields.astype(jnp.float32), everyone, coef_rows, dist_rows, target, valid_rows
    )
    partial_weight = jnp.einsum(
        "mvg,mgd->vd", grad_fields, hidden, preferred_element_type=jnp.float32
    )
    summed = lax.psum(partial_weight, ("member", "space"))
    column_count = latent_width // lax.axis_size("space")
    grad_w_out = lax.dynamic_slice_in_dim(summed, band_index * column_count, column_count, 1)
    back = jnp.einsum("vd,mvg->mgd", w_out, grad_fields, preferred_element_type=jnp.float32)
    sigmoid_part = jax.nn.sigmoid(preact)
    grad_pre = (back * sigmoid_part * (1.0 + preact * (1.0 - sigmoid_part))).astype(jnp.bfloat16)
    grad_mixed = jnp.einsum("mge,de->mgd", grad_pre, w_in, preferred_element_type=jnp.float32)
    spread_terms = (edge_weight[None, :, :, None] * grad_mixed[:, None]).reshape(
        members_dev, -1, latent_width
    )
    flat_index = local_index.reshape(-1)
    collected = jax.vmap(
        lambda edge_terms: jax.ops.segment_sum(edge_terms, flat_index, num_segments=3 * nodes_dev)
    )(spread_terms)
    lower_rim = collected[:, :nodes_dev].astype(jnp.bfloat16)
    middle_rows = collected[:, nodes_dev : 2 * nodes_dev]
    upper_rim = collected[:, 2 * nodes_dev :].astype(jnp.bfloat16)
    from_above = passed_along(lower_rim, "space", -1)
    from_below = passed_along(upper_rim, "space", 1)
    grad_latent = (
        middle_rows + from_above.astype(jnp.float32) + from_below.astype(jnp.float32)
    ).astype(jnp.bfloat16)
    return (score, grad_latent, grad_w_out)


def solution(mesh):
    return jax.shard_map(
        per_device,
        mesh=mesh,
        in_specs=(
            P("member", "space", None),
            P(None, "space"),
            P(None, "space"),
            P("space"),
            P(),
            P(),
            P(None, "space"),
        ),
        out_specs=(P(), P("member", "space", None), P(None, "space")),
        check_vma=False,
    )
```

profile of v0, /device:TPU:4, one launch (start us, length us, event | category | flops | bytes accessed | tf_op | source)
XLA Modules:
  0.0 1032.3 jit_solution(2826235210925329485)
XLA Ops:
  13.2 2.4 collective-permute-done.1
  17.6 41.8 %gather_fusion = bf16[1536,2,1024]{2,1,0:T(2,128)(2,1)} fusion(bf16[2,192,1024]{2,0,1:T(2,128)(2,1)S(1)} %pad_maximum_fusion, s32[2048]{0:T(1024)S(1)} %pad_clamp_fusion), kind=kCustom, calls=%fused_computation | custom fusion | bytes 12589056 | tf_op jit(solution)/shard_map/jit(_take)/gather | solution.py:66
  59.5 6.4 copy_select_fusion
  65.9 4.7 multiply_convert_fusion.1
  75.0 67.4 %all-gather.2.cloned.1.call-done = bf16[16,69,512]{2,1,0:T(8,128)(2,1)} async-done(((bf16[2,69,512]{2,1,0:T(8,128)(2,1)}), bf16[16,69,512]{2,1,0:T(8,128)(2,1)}) %all-gather.2.cloned.1.call-update) | async-done | bytes 1130512 | tf_op jit(solution)/shard_map/all_gather | solution.py:81
  142.3 3.0 convert_element_type.76
  145.4 59.9 %while.11 = (s32[]{:T(128)}, f32[16,16]{1,0:T(8,128)S(1)}, f32[16,69,512]{2,1,0:T(8,128)}, s32[]{:T(128)}, s32[]{:T(128)}, /*index=5*/s32[]{:T(128)}) while((s32[]{:T(128)}, f32[16,16]{1,0:T(8,128)S(1)}, f32[16,69,512]{2,1,0:T(8,128)}, s32[]{:T(128)}, s32[]{:T(128)}, /*index=5*/s32[]{:T(128)}) %tuple.38), condition=%wide.region_7.8_spmd.clone, body=%wide.region_5.7_spmd.clone.sunk | while | flops 2262002 | bytes 2689297 | solution.py:36
  147.0 2.1 fusion.44
  150.8 2.1 fusion.44
  154.5 2.1 fusion.44
  176.9 2.1 fusion.44
  180.7 2.1 fusion.44
  184.4 2.1 fusion.44
  188.2 2.1 fusion.44
  191.9 2.1 fusion.44
  195.6 2.1 fusion.44
  206.7 112.9 %all-reduce = (f32[16]{0:T(128)S(1)}, f32[]{:T(128)}, f32[16,16]{1,0:T(8,128)S(1)}) all-reduce(f32[16]{0:T(128)S(1)} %fusion.7, f32[]{:T(128)} %fusion.30, f32[16,16]{1,0:T(8,128)S(1)} %get-tuple-element.25), channel_id=1, replica_groups=mesh['member'=8,'space'=64] {'space'}, use_global_device_ids=true, to_apply=%region_1.2 | all-reduce | flops 273 | bytes 2184 | tf_op jit(solution)/shard_map/psum | solution.py:83
  323.2 7.9 fusion.10
  331.1 5.4 copy.33
  336.5 10.1 bitcast_multiply_fusion
  348.2 211.3 %scatter_fusion = f32[2,192,1024]{2,0,1:T(2,128)} fusion(f32[2,192,1024]{2,0,1:T(2,128)} %broadcast_in_dim.23, s32[1536]{0:T(1024)S(1)} %reshape.87, f32[1536,2,1024]{2,1,0:T(2,128)} %bitcast.66), kind=kCustom, calls=%fused_computation.1 | custom fusion | flops 3145728 | bytes 37754880 | tf_op jit(solution)/shard_map/vmap()/scatter-add | solution.py:106
  563.8 3.0 collective-permute-start.3
  566.9 3.4 convolution_bitcast_fusion
  571.6 449.3 %all-reduce.3.cloned.1.call-done = f32[69,1024]{0,1:T(8,128)} async-done(((f32[69,1024]{0,1:T(8,128)}), f32[69,1024]{0,1:T(8,128)}) %all-reduce.3.cloned.1.call-update) | async-done | bytes 282640 | tf_op jit(solution)/shard_map/psum | solution.py:94
  (103 shorter events, 65.9 us)
Async XLA Ops:
  7.2 58.7 %copy-start = (bf16[1024,1024]{1,0:T(8,128)(2,1)S(1)}, bf16[1024,1024]{1,0:T(8,128)(2,1)}, u32[]{:S(2)}) copy-start(bf16[1024,1024]{1,0:T(8,128)(2,1)} %param.13) | copy-start | bytes 6291460
  7.2 135.2 %all-gather.2.cloned.1.call-start = ((), (), s32[]{:S(2)}) async-start(), calls=%async_computation | async-start | bytes 1327104 | tf_op jit(solution)/shard_map/all_gather | solution.py:81
  8.6 4.7 collective-permute-start
  10.4 5.3 collective-permute-start.1
  65.9 6.1 copy-start.4
  65.9 7.8 copy-start.5
  70.6 1.4 copy-start.2
  73.4 947.4 %all-reduce.3.cloned.1.call-start = ((), (), s32[]{:S(2)}) async-start(), calls=%async_computation.1 | async-start | bytes 1048576 | tf_op jit(solution)/shard_map/psum | solution.py:94
  145.4 59.9 %copy-start.1 = (bf16[16,69,512]{2,1,0:T(8,128)(2,1)S(1)}, bf16[16,69,512]{2,1,0:T(8,128)(2,1)}, u32[]{:S(2)}) copy-start(bf16[16,69,512]{2,1,0:T(8,128)(2,1)} %all-gather.2.cloned.1.call-done) | copy-start | bytes 3391492
  205.3 117.9 %copy-start.3 = (bf16[2,69,512]{2,1,0:T(8,128)(2,1)S(1)}, bf16[2,69,512]{2,1,0:T(8,128)(2,1)}, u32[]{:S(2)}) copy-start(bf16[2,69,512]{2,1,0:T(8,128)(2,1)} %fusion.16) | copy-start | bytes 423940
  562.5 459.7 %collective-permute-start.2 = (bf16[2,64,1024]{2,0,1:T(2,128)(2,1)}, bf16[2,64,1024]{2,0,1:T(2,128)(2,1)S(1)}, u32[]{:S(2)}, u32[]{:S(2)}) collective-permute-start(bf16[2,64,1024]{2,0,1:T(2,128)(2,1)} %get-tuple-element.68), channel_id=1, source_target_pairs={{1,0},{2,1},{3,2},{4,3},{5,4},{6,5},{7,6},{8,7},{9,8},{10,9},{11,1... | collective-permute-start | bytes 786440 | tf_op jit(solution)/shard_map/ppermute | solution.py:25
  563.8 458.4 %collective-permute-start.3 = (bf16[2,64,1024]{2,0,1:T(2,128)(2,1)S(1)}, bf16[2,64,1024]{2,0,1:T(2,128)(2,1)S(1)}, u32[]{:S(2)}, u32[]{:S(2)}) collective-permute-start(bf16[2,64,1024]{2,0,1:T(2,128)(2,1)S(1)} %get-tuple-element.69), channel_id=1, source_target_pairs={{0,1},{1,2},{2,3},{3,4},{4,5},{5,6},{6,7},{7,8},{8,9},{9,10},{10,1... | collective-permute-start | bytes 786440 | tf_op jit(solution)/shard_map/ppermute | solution.py:25
Sparse Core Ops, SparseCore 0:
  73.6 68.7 all-gather.1
  570.4 450.4 all-reduce.2
where the time goes:
time: 1040 us; the launch traced here: 1030 us
  waiting for transfers between devices  519 us (50%)
  other arithmetic  286 us (28%)
  blocking collectives  113 us (11%)
  local copies, waits for them, and re-layouts  71.2 us (7%)
  between operations  18 us (2%)
  matrix products  17.5 us (2%)
    psum x1, waiting for transfers between devices, per_device(): summed = lax.psum(partial_weight, ('member', 'space'))  449 us
    scatter-add x1, other arithmetic, per_device(): jax.ops.segment_sum(edge_terms, flat_index, num_segments=3 * nodes_dev)  211 us
    psum x1, blocking collectives, per_device(): lax.psum((target_sums, pair_sums, cell_count), 'space')  113 us
    all_gather x1, waiting for transfers between devices, per_device(): lax.all_gather(fields, 'member', axis=0, tiled=True).astype(jnp.float32)  67.4 us
    gather x1, local copies, waits for them, and re-layouts, per_device(): jnp.take(extended, local_index.reshape(-1), axis=1)  41.8 us
    reduce_sum x16, other arithmetic, against(): return jnp.sum(valid_rows * spread * spread, axis=(1, 2))  33.9 us
  transfers between devices with their start and end apart: 6, of which 3 were waited for; matrix products, arithmetic and copies ran while one was open for 1% of the time, Pallas kernels for 0%

commit v1 on v0

--- a/solution.py
+++ b/solution.py
@@ -78,7 +78,9 @@
         jnp.bfloat16
     )
     valid_rows = (jnp.arange(row_count) < band_rows[0]).astype(jnp.float32)
-    everyone = lax.all_gather(fields, "member", axis=0, tiled=True).astype(jnp.float32)
+    everyone = jnp.concatenate(
+        lax.all_to_all(jnp.stack([fields] * lax.axis_size("member")), "member", 0, 0), axis=0
+    ).astype(jnp.float32)
     target_sums, pair_sums, cell_count = partials(everyone, target, valid_rows)
     target_sums, pair_sums, cell_count = lax.psum((target_sums, pair_sums, cell_count), "space")
     score, pair_coef, target_dist = finish(target_sums, pair_sums, cell_count, variables)

time: 1040 us -> 1000 us (0.962)
  waiting for transfers between devices: 519 us -> 467 us
    all_gather x1 -> x0, waiting for transfers between devices: 67.4 us -> none  [per_device(): lax.all_gather(fields, 'member', axis=0, tiled=True).astype(jnp.float32)]
    all_to_all x0 -> x1, waiting for transfers between devices: none -> 11.6 us  [per_device(): lax.all_to_all(jnp.stack([fields] * lax.axis_size('member')), 'member', 0...]
where the time goes in v1:
time: 1000 us
  waiting for transfers between devices  467 us (47%)
  other arithmetic  285 us (28%)
  blocking collectives  122 us (12%)
  local copies, waits for them, and re-layouts  76.7 us (8%)
  between operations  18 us (2%)
  matrix products  16.5 us (2%)
  starting transfers between devices  15 us (2%)
    psum x1, waiting for transfers between devices, per_device(): summed = lax.psum(partial_weight, ('member', 'space'))  453 us
    scatter-add x1, other arithmetic, per_device(): jax.ops.segment_sum(edge_terms, flat_index, num_segments=3 * nodes_dev)  211 us
    psum x1, blocking collectives, per_device(): lax.psum((target_sums, pair_sums, cell_count), 'space')  122 us
    gather x1, local copies, waits for them, and re-layouts, per_device(): jnp.take(extended, local_index.reshape(-1), axis=1)  41.8 us
    reduce_sum x16, other arithmetic, against(): return jnp.sum(valid_rows * spread * spread, axis=(1, 2))  33.9 us
  transfers between devices with their start and end apart: 6, of which 3 were waited for; matrix products, arithmetic and copies ran while one was open for 1% of the time, Pallas kernels for 0%

profile of v1, /device:TPU:4, one launch (start us, length us, event | category | flops | bytes accessed | tf_op | source)
XLA Modules:
  0.0 999.9 jit_solution(6535308230931956038)
XLA Ops:
  13.2 2.4 collective-permute-done.1
  17.6 41.8 %gather_fusion = bf16[1536,2,1024]{2,1,0:T(2,128)(2,1)} fusion(bf16[2,192,1024]{2,0,1:T(2,128)(2,1)S(1)} %pad_maximum_fusion, s32[2048]{0:T(1024)S(1)} %pad_clamp_fusion), kind=kCustom, calls=%fused_computation | custom fusion | bytes 12589056 | tf_op jit(solution)/shard_map/jit(_take)/gather | solution.py:66
  59.4 6.4 copy_select_fusion
  65.8 4.7 multiply_convert_fusion.1
  74.4 7.6 all-to-all-start
  83.3 11.6 %all-to-all-done = bf16[8,2,69,512]{3,1,2,0:T(2,128)(2,1)S(1)} async-done(((bf16[8,2,69,512]{3,1,2,0:T(2,128)(2,1)}), bf16[8,2,69,512]{3,1,2,0:T(2,128)(2,1)S(1)}, u32[]{:S(2)}, u32[]{:S(2)}) %all-to-all-start) | async-done | bytes 1130528 | tf_op jit(solution)/shard_map/all_to_all | solution.py:82
  98.2 2.7 copy.67
  100.9 59.8 %while.11 = (s32[]{:T(128)}, f32[16,16]{1,0:T(8,128)S(1)}, f32[16,69,512]{2,1,0:T(8,128)}, s32[]{:T(128)}, s32[]{:T(128)}, /*index=5*/s32[]{:T(128)}) while((s32[]{:T(128)}, f32[16,16]{1,0:T(8,128)S(1)}, f32[16,69,512]{2,1,0:T(8,128)}, s32[]{:T(128)}, s32[]{:T(128)}, /*index=5*/s32[]{:T(128)}) %tuple.47), condition=%wide.region_7.8_spmd.clone, body=%wide.region_5.7_spmd.clone.sunk | while | flops 2262002 | bytes 2689297 | solution.py:36
  102.6 2.1 fusion.44
  106.3 2.1 fusion.44
  110.0 2.1 fusion.44
  113.8 2.1 fusion.44
  117.5 2.1 fusion.44
  121.3 2.1 fusion.44
  125.0 2.1 fusion.44
  160.8 121.9 %all-reduce = (f32[16]{0:T(128)S(1)}, f32[]{:T(128)}, f32[16,16]{1,0:T(8,128)S(1)}) all-reduce(f32[16]{0:T(128)S(1)} %reduce_sum.66, f32[]{:T(128)} %fusion.30, f32[16,16]{1,0:T(8,128)S(1)} %get-tuple-element.25), channel_id=1, replica_groups=mesh['member'=8,'space'=64] {'space'}, use_global_device_ids=true, to_apply=%region_1.2 | all-reduce | flops 273 | bytes 2184 | tf_op jit(solution)/shard_map/psum | solution.py:85
  284.8 2.7 multiply_reduce_fusion
  287.5 7.7 fusion.10
  295.2 5.4 copy.68
  300.6 10.1 %bitcast_multiply_fusion = f32[2,1536,1024]{2,0,1:T(2,128)} fusion(f32[1536]{0:T(1024)S(1)} %mul.145, f32[2,512,1024]{2,0,1:T(2,128)S(1)} %copy.68), kind=kLoop, calls=%fused_computation.8 | loop fusion | flops 3145728 | bytes 16783360 | tf_op jit(solution)/shard_map/mul | solution.py:103
  312.3 211.3 %scatter_fusion = f32[2,192,1024]{2,0,1:T(2,128)} fusion(f32[2,192,1024]{2,0,1:T(2,128)} %broadcast_in_dim.23, s32[1536]{0:T(1024)S(1)} %reshape.98, f32[1536,2,1024]{2,1,0:T(2,128)} %bitcast.69), kind=kCustom, calls=%fused_computation.1 | custom fusion | flops 3145728 | bytes 37754880 | tf_op jit(solution)/shard_map/vmap()/scatter-add | solution.py:108
  527.9 3.0 collective-permute-start.3
  531.0 3.3 convolution_bitcast_fusion
  535.7 452.8 %all-reduce.3.cloned.1.call-done = f32[69,1024]{0,1:T(8,128)} async-done(((f32[69,1024]{0,1:T(8,128)}), f32[69,1024]{0,1:T(8,128)}) %all-reduce.3.cloned.1.call-update) | async-done | bytes 282640 | tf_op jit(solution)/shard_map/psum | solution.py:96
  (111 shorter events, 71.2 us)
Async XLA Ops:
  7.2 58.6 %copy-start = (bf16[1024,1024]{1,0:T(8,128)(2,1)S(1)}, bf16[1024,1024]{1,0:T(8,128)(2,1)}, u32[]{:S(2)}) copy-start(bf16[1024,1024]{1,0:T(8,128)(2,1)} %param.13) | copy-start | bytes 6291460
  8.6 4.7 collective-permute-start
  10.3 5.3 collective-permute-start.1
  65.8 6.1 copy-start.3
  70.6 1.4 copy-start.2
  70.6 11.5 %copy-start.6 = (f32[3,512]{1,0:T(4,128)S(1)}, f32[3,512]{1,0:T(4,128)}, u32[]{:S(2)}) copy-start(f32[3,512]{1,0:T(4,128)} %param.10) | copy-start | bytes 18436
  74.4 20.5 %all-to-all-start = ((bf16[8,2,69,512]{3,1,2,0:T(2,128)(2,1)}), bf16[8,2,69,512]{3,1,2,0:T(2,128)(2,1)S(1)}, u32[]{:S(2)}, u32[]{:S(2)}) async-start(bf16[8,2,69,512]{3,1,2,0:T(2,128)(2,1)} %stack.2), calls=%async_computation | async-start | bytes 2260992 | tf_op jit(solution)/shard_map/all_to_all | solution.py:82
  82.0 906.5 %all-reduce.3.cloned.1.call-start = ((), (), s32[]{:S(2)}) async-start(), calls=%async_computation.1 | async-start | bytes 1048576 | tf_op jit(solution)/shard_map/psum | solution.py:96
  96.8 4.1 copy-start.7
  98.2 2.8 copy-start.1
  100.9 186.5 %copy-start.4 = (f32[69,512]{1,0:T(8,128)S(1)}, f32[69,512]{1,0:T(8,128)}, u32[]{:S(2)}) copy-start(f32[69,512]{1,0:T(8,128)} %param.15) | copy-start | bytes 423940
  312.3 218.7 %copy-start.5 = (f32[69,512]{1,0:T(8,128)S(1)}, f32[69,512]{1,0:T(8,128)}, u32[]{:S(2)}) copy-start(f32[69,512]{1,0:T(8,128)} %param.15) | copy-start | bytes 423940
  526.6 463.1 %collective-permute-start.2 = (bf16[2,64,1024]{2,0,1:T(2,128)(2,1)}, bf16[2,64,1024]{2,0,1:T(2,128)(2,1)S(1)}, u32[]{:S(2)}, u32[]{:S(2)}) collective-permute-start(bf16[2,64,1024]{2,0,1:T(2,128)(2,1)} %get-tuple-element.77), channel_id=1, source_target_pairs={{1,0},{2,1},{3,2},{4,3},{5,4},{6,5},{7,6},{8,7},{9,8},{10,9},{11,1... | collective-permute-start | bytes 786440 | tf_op jit(solution)/shard_map/ppermute | solution.py:25
  527.9 461.9 %collective-permute-start.3 = (bf16[2,64,1024]{2,0,1:T(2,128)(2,1)S(1)}, bf16[2,64,1024]{2,0,1:T(2,128)(2,1)S(1)}, u32[]{:S(2)}, u32[]{:S(2)}) collective-permute-start(bf16[2,64,1024]{2,0,1:T(2,128)(2,1)S(1)} %get-tuple-element.78), channel_id=1, source_target_pairs={{0,1},{1,2},{2,3},{3,4},{4,5},{5,6},{6,7},{7,8},{8,9},{9,10},{10,1... | collective-permute-start | bytes 786440 | tf_op jit(solution)/shard_map/ppermute | solution.py:25
Sparse Core Ops, SparseCore 0:
  534.5 453.9 all-reduce.2
